TPU v7x, 32 devices: a whole 2x2x4 slice. The times are simulated.
32 devices in a mesh: groups: 2 (over x), range: 16 (over z, y, core).
Axes of the slice: x: 2, y: 2, z: 4, core: 2. Of those that a mesh axis runs over, the one named last changes fastest.
Arguments:
- echoes: bfloat16 [4, 256, 16384], P('groups', 'range'), parts along dimension 0, may hold values from -6 to 6
- range_reference: float32 [2, 16384], replicated, may hold values from -6 to 6
- kernels: float32 [16, 8], replicated, may hold values from -2 to 2
- shifts: int32 [128, 256], P('range'), may hold values from 0 to 12
- phase_index: int32 [128, 256], P('range'), may hold values from 0 to 15
- centroid: int32 [128], P('range'), may hold values from 0 to 255
- azimuth_reference: float32 [2, 128, 256], P(None, 'range'), may hold values from -6 to 6
Outputs:
- focused_image: bfloat16 [4, 256, 16384], P('groups', None, 'range'), parts along dimension 0
There are 2 independent parts, one for each index of `groups`. A program takes and returns all parts, laid end to end along the dimension named above; an argument that names none is the same for every part. Nothing has to cross between parts.
Inputs may be any that keep to these rules, and one draw needn't show every extreme that they name: `shifts`: whole range cells by which a block's energy at a Doppler bin has migrated. `phase_index`: row of kernels used by a block at a Doppler bin. `centroid`: doppler bins by which a block's azimuth reference is turned.
All inputs are finite; a program needn't handle non-finite values.
Results may differ from a plain program's by a relative error of at most 0.014.
Values may be sent and summed in bfloat16 or wider, within the bound.
A program may use at most 128 MiB of HBM per device.

v0:
```python
import functools
import math

import jax
import jax.numpy as jnp
import ml_dtypes
import numpy as np
from jax import lax
from jax.experimental import pallas as pl
from jax.experimental.pallas import tpu as pltpu
from jax.sharding import PartitionSpec as P

R1 = 128
RB = 128
F32 = jnp.float32
BF16 = jnp.bfloat16
VMEM_BYTES = 58 << 20


def roots(length, orient):
    line = np.arange(length)
    angles = 2.0 * math.pi / length * (line[:, None] * line[None, :] % length)
    rounded = lambda part: part.astype(ml_dtypes.bfloat16).astype(np.float64)
    return rounded(np.cos(angles)) + 1j * orient * rounded(np.sin(angles))


def twist(first_len, second_len, orient):
    whole = first_len * second_len
    turns = np.arange(first_len)[:, None] * np.arange(second_len)[None, :] % whole
    return np.exp(orient * 2j * math.pi / whole * turns)


def left_matrix(m):
    return np.block([[m.real, -m.imag], [m.imag, m.real]]).astype(ml_dtypes.bfloat16)


def right_matrix(m):
    return np.block([[m.real, m.imag], [-m.imag, m.real]]).astype(ml_dtypes.bfloat16)


def pair(m):
    return np.stack([m.real, m.imag]).astype(np.float32)


def azimuth_matrix(first, second):
    parts = np.einsum(
        "ka,mk,bm->bkam", roots(first, -1.0), twist(second, first, -1.0), roots(second, -1.0)
    )
    return parts.reshape(first * second, first * second) / math.sqrt(first * second)


def dot(a, b):
    return jnp.dot(a, b, preferred_element_type=F32)


def fetch(pairs, sems):
    copies = [pltpu.make_async_copy(src, dst, sems.at[i]) for i, (src, dst) in enumerate(pairs)]
    for copy in copies:
        copy.start()
    return copies


def range_kernel(
    ranks, group, e_hbm, ref_hbm, mats_hbm, tables_hbm, send_ref,
    lines, cells, slots, e_ref, ref_ref, mats, tables, sems,
):
    pulses = e_ref.shape[1]
    blocks = R1 // ranks
    copies = fetch(
        [(e_hbm, e_ref), (ref_hbm, ref_ref), (tables_hbm, tables), (mats_hbm, mats)], sems
    )
    copies[0].wait()

    def spread(n1, carry):
        lane = pl.multiple_of(n1 * RB, RB)
        for part in range(2):
            lines[part, pl.ds(n1, pulses, stride=R1), :] = e_ref[part, :, pl.ds(lane, RB)].astype(F32)
        return carry

    lax.fori_loop(0, R1, spread, 0, unroll=8)
    for copy in copies[1:]:
        copy.wait()
    for part in range(2):
        for k2 in range(ref_ref.shape[1] // R1):
            slots[part, k2 : k2 + 1, :] = ref_ref[part : part + 1, k2 * R1 : (k2 + 1) * R1]
    for part in range(2):
        slots[part] = slots[part].T

    def times(re, im, tr, ti):
        return (re * tr - im * ti).astype(BF16), (re * ti + im * tr).astype(BF16)

    def step(g, carry):
        def line(part, j):
            return lines[part, pl.ds(pl.multiple_of((g * group + j) * R1, R1), R1), :].astype(BF16)

        x = jnp.concatenate(
            [jnp.concatenate([line(part, j) for j in range(group)], 1) for part in range(2)], 0
        )
        u = dot(mats[0], x)
        tr, ti = tables[0], tables[1]
        u = jnp.concatenate(
            [
                jnp.concatenate(
                    times(u[:R1, j * RB : (j + 1) * RB], u[R1:, j * RB : (j + 1) * RB], tr, ti), 1
                )
                for j in range(group)
            ],
            0,
        )
        s = dot(u, mats[1])
        tr, ti = slots[0], slots[1]
        s = jnp.concatenate(
            [
                jnp.concatenate(
                    times(s[j * R1 : (j + 1) * R1, :RB], s[j * R1 : (j + 1) * R1, RB:], tr, ti), 1
                )
                for j in range(group)
            ],
            0,
        )
        v = dot(s, mats[2])
        tr, ti = tables[2], tables[3]
        v = jnp.concatenate(
            [
                jnp.concatenate(
                    times(v[j * R1 : (j + 1) * R1, :RB], v[j * R1 : (j + 1) * R1, RB:], tr, ti), 0
                )
                for j in range(group)
            ],
            1,
        )
        r = dot(mats[3], v)
        for j in range(group):
            for part in range(2):
                cells[part, pl.ds(g * group + j, R1, stride=pulses), :] = r[
                    part * R1 : (part + 1) * R1, j * RB : (j + 1) * RB
                ]
        return carry

    lax.fori_loop(0, pulses // group, step, 0)

    lane = lax.broadcasted_iota(jnp.int32, (pulses, RB), 1)
    mine = (lane < RB // 4) | (lane >= RB - RB // 4)
    zero = jnp.zeros((pulses, RB), F32)

    for d in range(ranks):
        packed = []
        for part in range(2):
            after = zero if d == ranks - 1 else cells[part, pl.ds((d + 1) * blocks * pulses, pulses), :]
            before = zero if d == 0 else cells[part, pl.ds((d * blocks - 1) * pulses, pulses), :]
            packed.append(jnp.where(lane < RB // 2, after, before))
        send_ref[d, :pulses, :] = jnp.where(
            mine, packed[0], pltpu.roll(packed[1], RB // 2, 1)
        ).astype(BF16)
        for b in range(blocks):
            for part in range(2):
                begin = pulses + (2 * b + part) * pulses
                send_ref[d, begin : begin + pulses, :] = cells[
                    part, pl.ds((d * blocks + b) * pulses, pulses), :
                ].astype(BF16)


def turn_kernel(
    ranks, chunk, send_hbm, kernels_hbm, shift_hbm, phase_hbm, az_hbm, ahead_hbm, centroid_ref,
    out_ref, got, doppler, weights, filters, moves,
    kernels_ref, shift_ref, phase_ref, az_ref, ahead, sems, send_sems, got_sems,
):
    me = lax.axis_index("range")
    blocks, total = shift_ref.shape
    pulses = total // ranks
    taps, phases = kernels_ref.shape
    lead = taps // 2 - 1
    chunks = blocks // chunk

    barrier = pltpu.get_barrier_semaphore()

    def greet(k, carry):
        pl.semaphore_signal(
            barrier, inc=1, device_id={"range": lax.rem(me + k, ranks)},
            device_id_type=pl.DeviceIdType.MESH,
        )
        return carry

    lax.fori_loop(1, ranks, greet, 0)
    copies = fetch(
        [
            (kernels_hbm, kernels_ref), (shift_hbm, shift_ref), (phase_hbm, phase_ref),
            (az_hbm, az_ref), (ahead_hbm, ahead), (send_hbm.at[me], got.at[me]),
        ],
        sems,
    )
    pl.semaphore_wait(barrier, ranks - 1)

    def rows(c):
        if c == 0:
            return pl.ds(0, pulses + 2 * chunk * pulses)
        return pl.ds(pulses + 2 * c * chunk * pulses, 2 * chunk * pulses)

    def remote(c, to, owner):
        return pltpu.make_async_remote_copy(
            src_ref=send_hbm.at[to, rows(c)],
            dst_ref=got.at[owner, rows(c)],
            send_sem=send_sems.at[c, to],
            recv_sem=got_sems.at[c, owner],
            device_id={"range": to},
            device_id_type=pl.DeviceIdType.MESH,
        )

    half = ranks // 2
    for c in range(chunks):

        def begin(k, carry):
            remote(c, lax.rem(me + k, ranks), me).start()
            return carry

        lax.fori_loop(half, ranks, begin, 0)
        lax.fori_loop(1, half, begin, 0)

    for copy in copies:
        copy.wait()

    wide = lax.broadcasted_iota(jnp.int32, (blocks, 1), 0)
    turns = jnp.zeros((blocks, 1), jnp.int32)
    for b in range(blocks):
        turns = jnp.where(wide == b, centroid_ref[b], turns)
    turns = jnp.broadcast_to(turns, (blocks, total))
    lines = []
    for part in range(2):
        line = az_ref[part]
        step = 1
        while step < total:
            line = jnp.where((turns & step) != 0, pltpu.roll(line, step, 1), line)
            step *= 2
        lines.append(line)
    lines.append(shift_ref[...].astype(F32))
    lines.append(phase_ref[...].astype(F32))
    lines.append(jnp.zeros((RB - 4 * blocks, total), F32))
    columns = jnp.concatenate(lines, 0).T

    def column(j):
        return jnp.broadcast_to(columns[:, j : j + 1], (total, RB))

    left = jnp.concatenate([kernels_ref[...], jnp.zeros((taps, RB - phases), F32)], 1).T
    terms = []
    for _ in range(3):
        term = left.astype(BF16)
        left = left - term.astype(F32)
        terms.append(term[:phases])
    terms.append(jnp.zeros((RB - 3 * phases, taps), BF16))
    table = jnp.concatenate(terms, 0).astype(F32)
    table = jnp.concatenate(
        [jnp.broadcast_to(table[:, t : t + 1], (RB, RB)) for t in range(taps)], 1
    ).astype(BF16)
    slot = lax.broadcasted_iota(jnp.int32, (total, RB), 1)
    slot = jnp.where(slot < 3 * phases, lax.rem(slot, phases), -1)

    for b in range(blocks):
        filters[b, 0] = column(b)
        filters[b, 1] = column(blocks + b)
        moves[b] = column(2 * blocks + b).astype(jnp.int32)
        chosen = jnp.where(column(3 * blocks + b).astype(jnp.int32) == slot, 1.0, 0.0).astype(BF16)
        for t in range(0, taps, 2):
            pair_of = dot(chosen, table[:, t * RB : (t + 2) * RB])
            weights[b, t] = pair_of[:, :RB]
            weights[b, t + 1] = pair_of[:, RB:]

    size = 32
    lane = lax.broadcasted_iota(jnp.int32, (size, RB), 1)

    def focus(b):
        for row in range(0, total, size):
            here = pl.ds(row, size)
            shift = moves[b, here, :]
            where = (lane + shift + (RB - lead)) & (RB - 1)
            early = lane < RB - shift
            found = []
            for part in range(2):
                at = pl.ds(part * total + row, size)
                prev, cur, after = doppler[b, at, :], doppler[b + 1, at, :], doppler[b + 2, at, :]
                a = jnp.take_along_axis(jnp.where(lane >= RB - lead, prev, cur), where, axis=1)
                z = jnp.take_along_axis(jnp.where(lane >= RB - lead, cur, after), where, axis=1)
                x = jnp.where(early, a, z)
                summed = weights[b, 0, here, :] * x
                for t in range(1, taps):
                    summed += weights[b, t, here, :] * pltpu.roll(jnp.where(lane < t, z, x), RB - t, 1)
                found.append(summed)
            ar, ai = filters[b, 0, here, :], filters[b, 1, here, :]
            cells = pl.ds(b * RB, RB)
            out_ref[here, cells] = (found[0] * ar - found[1] * ai).astype(BF16)
            out_ref[pl.ds(total + row, size), cells] = (found[0] * ai + found[1] * ar).astype(BF16)

    for c in range(chunks):

        def arrive(k, carry):
            remote(c, me, lax.rem(me + k, ranks)).wait_recv()
            return carry

        lax.fori_loop(1, ranks, arrive, 0)
        if c == 0:
            halo = got[:, :pulses, :]
            turned = jnp.concatenate([halo[:, :, RB // 2 :], halo[:, :, : RB // 2]], 2)
            edge = jnp.stack([halo, turned], 1).reshape(2 * total, RB)
            edge = dot(ahead[...], edge)
            doppler[0] = edge
            doppler[blocks + 1] = edge
        for b in range(c * chunk, (c + 1) * chunk):
            begin_row = pulses + 2 * b * pulses
            x = got[:, begin_row : begin_row + 2 * pulses, :].reshape(2 * total, RB)
            doppler[b + 1] = dot(ahead[...], x)
        for b in range(max(c * chunk - 1, 0), (c + 1) * chunk - (c < chunks - 1)):
            focus(b)

    for c in range(chunks):

        def leave(k, carry):
            remote(c, lax.rem(me + k, ranks), me).wait_send()
            return carry

        lax.fori_loop(1, ranks, leave, 0)


def local(echoes, range_reference, kernels, shifts, phase_index, centroid, azimuth_reference):
    ranks = lax.axis_size("range")
    pulses, samples = echoes.shape[1:]
    second = samples // R1
    blocks = R1 // ranks
    total = ranks * pulses
    taps = kernels.shape[1]
    mats = np.stack([
        left_matrix(roots(R1, -1.0)),
        right_matrix(roots(second, -1.0)),
        right_matrix(roots(second, 1.0)),
        left_matrix(roots(R1, 1.0)),
    ])
    tables = np.concatenate([
        pair(twist(R1, second, -1.0) / math.sqrt(samples)),
        pair(twist(R1, second, 1.0) / math.sqrt(samples)),
    ])
    turn = azimuth_matrix(ranks, pulses)
    ahead = left_matrix(turn).reshape(2 * total, 2, ranks, pulses).transpose(0, 2, 1, 3)
    ahead = ahead.reshape(2 * total, 2 * total)
    back = left_matrix(turn.conj().T)
    vmem = pl.BlockSpec(memory_space=pltpu.VMEM)
    anywhere = pl.BlockSpec(memory_space=pl.ANY)
    height = 2 * blocks * pulses + pulses
    dma = pltpu.SemaphoreType.DMA
    send = pl.pallas_call(
        functools.partial(range_kernel, ranks, math.gcd(pulses, 4)),
        out_shape=jax.ShapeDtypeStruct((ranks, height, RB), BF16),
        in_specs=[anywhere] * 4,
        out_specs=vmem,
        scratch_shapes=[
            pltpu.VMEM((2, R1 * pulses, RB), F32),
            pltpu.VMEM((2, R1 * pulses, RB), F32),
            pltpu.VMEM((2, R1, second), F32),
            pltpu.VMEM(echoes.shape, BF16),
            pltpu.VMEM(range_reference.shape, F32),
            pltpu.VMEM(mats.shape, BF16),
            pltpu.VMEM(tables.shape, F32),
            dma((4,)),
        ],
        compiler_params=pltpu.CompilerParams(vmem_limit_bytes=VMEM_BYTES),
        name="range_lines",
    )(echoes, range_reference, mats, tables)
    chunk = max(1, blocks // 4)
    focused = pl.pallas_call(
        functools.partial(turn_kernel, ranks, chunk),
        out_shape=jax.ShapeDtypeStruct((2 * total, blocks * RB), BF16),
        in_specs=[anywhere] * 6 + [pl.BlockSpec(memory_space=pltpu.SMEM)],
        out_specs=vmem,
        scratch_shapes=[
            pltpu.VMEM((ranks, height, RB), BF16),
            pltpu.VMEM((blocks + 2, 2 * total, RB), F32),
            pltpu.VMEM((blocks, taps, total, RB), F32),
            pltpu.VMEM((blocks, 2, total, RB), F32),
            pltpu.VMEM((blocks, total, RB), jnp.int32),
            pltpu.VMEM(kernels.shape[::-1], F32),
            pltpu.VMEM(shifts.shape, jnp.int32),
            pltpu.VMEM(shifts.shape, jnp.int32),
            pltpu.VMEM(azimuth_reference.shape, F32),
            pltpu.VMEM(ahead.shape, BF16),
            dma((6,)),
            dma((blocks // chunk, ranks)),
            dma((blocks // chunk, ranks)),
        ],
        compiler_params=pltpu.CompilerParams(
            vmem_limit_bytes=VMEM_BYTES, collective_id=0, has_side_effects=True
        ),
        name="turn_and_azimuth",
    )(send, kernels.T, shifts, phase_index, azimuth_reference, ahead, centroid)
    return dot(back, focused).astype(BF16).reshape(2, total, blocks * RB)


def solution(mesh):
    in_specs = (
        P("groups", "range", None),
        P(),
        P(),
        P("range", None),
        P("range", None),
        P("range"),
        P(None, "range", None),
    )
    out_specs = P("groups", None, "range")
    return jax.shard_map(local, mesh=mesh, in_specs=in_specs, out_specs=out_specs, check_vma=False)
```

profile of v0, /device:TPU:0, one launch (start us, length us, event | category | flops | bytes accessed | tf_op | source)
XLA Modules:
  0.0 52.1 jit_solution(3631354141460049098)
XLA Ops:
  0.0 8.0 %range_lines.1.send_hbm = bf16[16,272,128]{2,1,0:T(8,128)(2,1)} custom-call(bf16[2,16,16384]{2,1,0:T(8,128)(2,1)} %e_hbm.1, f32[2,16384]{1,0:T(2,128)} %ref_hbm.1, bf16[4,256,256]{2,1,0:T(8,128)(2,1)} %constant.8.clone.mats_hbm, f32[4,128,128]{2,1,0:T(8,128)} %constant.9.clone.tables_hbm), custom_call_target="tpu_custom_call" | custom-call | tf_op jit(solution)/shard_map/range_lines/pallas_call | solution.py:347
  8.1 0.0 copy-start
  8.1 41.1 %turn_and_azimuth.1 = bf16[512,1024]{1,0:T(8,128)(2,1)} custom-call(bf16[16,272,128]{2,1,0:T(8,128)(2,1)} %range_lines.1.send_hbm, f32[8,16]{1,0:T(8,128)} %bitcast.6, s32[8,256]{1,0:T(8,128)} %shift_hbm.1, s32[8,256]{1,0:T(8,128)} %phase_hbm.1, f32[2,8,256]{2,1,0:T(8,128)} %az_hbm.1, bf16[512,512]{1,0:T(8,128)(2,1)} %constant.10.clone.ahead_hbm, s32[8]{0:T(128)} %centroid_ref.1), custom_call_target="tpu_custom_call" | custom-call | tf_op jit(solution)/shard_map/turn_and_azimuth/pallas_call | solution.py:366
  49.2 0.0 copy-done
  49.2 2.9 %convolution_convert_fusion = bf16[1024,512]{0,1:T(8,128)(2,1)} fusion(bf16[512,512]{1,0:T(8,128)(2,1)S(1)} %copy-done, bf16[512,1024]{1,0:T(8,128)(2,1)} %turn_and_azimuth.1), kind=kOutput, calls=%fused_computation | convolution fusion | flops 537395200 | bytes 2621440 | tf_op jit(solution)/shard_map/dot_general | solution.py:53
Async XLA Ops:
  8.1 41.1 %copy-start = (bf16[512,512]{1,0:T(8,128)(2,1)S(1)}, bf16[512,512]{1,0:T(8,128)(2,1)}, u32[]{:S(2)}) copy-start(bf16[512,512]{1,0:T(8,128)(2,1)} %constant.11.clone) | copy-start | bytes 1572868
where the time goes:
time: 52.3 us; the launch traced here: 52.1 us
  Pallas kernels  49.1 us (94%)
  matrix products  2.91 us (6%)
    pallas_call x1, Pallas kernels, local(): pl.pallas_call(functools.partial(turn_kernel, ranks, chunk), out_shape=ja...  41.1 us
    pallas_call x1, Pallas kernels, local(): pl.pallas_call(functools.partial(range_kernel, ranks, math.gcd(pulses, 4)...  8.05 us
    dot_general x1, matrix products, dot(): return jnp.dot(a, b, preferred_element_type=F32)  2.91 us

commit v1 on v0

--- a/solution.py
+++ b/solution.py
@@ -77,7 +77,7 @@
             lines[part, pl.ds(n1, pulses, stride=R1), :] = e_ref[part, :, pl.ds(lane, RB)].astype(F32)
         return carry
 
-    lax.fori_loop(0, R1, spread, 0, unroll=8)
+    lax.fori_loop(0, R1, spread, 0, unroll=32)
     for copy in copies[1:]:
         copy.wait()
     for part in range(2):
@@ -91,7 +91,7 @@
 
     def step(g, carry):
         def line(part, j):
-            return lines[part, pl.ds(pl.multiple_of((g * group + j) * R1, R1), R1), :].astype(BF16)
+            return lines[part, pl.ds((g * group + j) * R1, R1), :].astype(BF16)
 
         x = jnp.concatenate(
             [jnp.concatenate([line(part, j) for j in range(group)], 1) for part in range(2)], 0
@@ -137,7 +137,8 @@
                 ]
         return carry
 
-    lax.fori_loop(0, pulses // group, step, 0)
+    for g in range(pulses // group):
+        step(g, 0)
 
     lane = lax.broadcasted_iota(jnp.int32, (pulses, RB), 1)
     mine = (lane < RB // 4) | (lane >= RB - RB // 4)
@@ -207,14 +208,17 @@
         )
 
     half = ranks // 2
-    for c in range(chunks):
-
+
+    def depart(c):
         def begin(k, carry):
             remote(c, lax.rem(me + k, ranks), me).start()
             return carry
 
         lax.fori_loop(half, ranks, begin, 0)
         lax.fori_loop(1, half, begin, 0)
+
+    for c in range(min(2, chunks)):
+        depart(c)
 
     for copy in copies:
         copy.wait()
@@ -296,6 +300,8 @@
             return carry
 
         lax.fori_loop(1, ranks, arrive, 0)
+        if c + 2 < chunks:
+            depart(c + 2)
         if c == 0:
             halo = got[:, :pulses, :]
             turned = jnp.concatenate([halo[:, :, RB // 2 :], halo[:, :, : RB // 2]], 2)

time: 52.3 us -> 51 us (0.975)
  Pallas kernels: 49.1 us -> 47.8 us
    pallas_call x1, Pallas kernels: 8.05 us -> 7.2 us  [local(): pl.pallas_call(functools.partial(range_kernel, ranks, math.gcd(pulses, 4)...]
where the time goes in v1:
time: 51 us; the launch traced here: 50.8 us
  Pallas kernels  47.8 us (94%)
  matrix products  2.91 us (6%)
    pallas_call x1, Pallas kernels, local(): pl.pallas_call(functools.partial(turn_kernel, ranks, chunk), out_shape=ja...  40.6 us
    pallas_call x1, Pallas kernels, local(): pl.pallas_call(functools.partial(range_kernel, ranks, math.gcd(pulses, 4)...  7.2 us
    dot_general x1, matrix products, dot(): return jnp.dot(a, b, preferred_element_type=F32)  2.91 us

profile of v1, /device:TPU:0, one launch (start us, length us, event | category | flops | bytes accessed | tf_op | source)
XLA Modules:
  0.0 50.8 jit_solution(1274700510093604647)
XLA Ops:
  0.0 7.2 %range_lines.1.send_hbm = bf16[16,272,128]{2,1,0:T(8,128)(2,1)} custom-call(bf16[2,16,16384]{2,1,0:T(8,128)(2,1)} %e_hbm.1, f32[2,16384]{1,0:T(2,128)} %ref_hbm.1, bf16[4,256,256]{2,1,0:T(8,128)(2,1)} %constant.8.clone.mats_hbm, f32[4,128,128]{2,1,0:T(8,128)} %constant.9.clone.tables_hbm), custom_call_target="tpu_custom_call" | custom-call | tf_op jit(solution)/shard_map/range_lines/pallas_call | solution.py:353
  7.2 0.0 copy-start
  7.2 40.6 %turn_and_azimuth.1 = bf16[512,1024]{1,0:T(8,128)(2,1)} custom-call(bf16[16,272,128]{2,1,0:T(8,128)(2,1)} %range_lines.1.send_hbm, f32[8,16]{1,0:T(8,128)} %bitcast.6, s32[8,256]{1,0:T(8,128)} %shift_hbm.1, s32[8,256]{1,0:T(8,128)} %phase_hbm.1, f32[2,8,256]{2,1,0:T(8,128)} %az_hbm.1, bf16[512,512]{1,0:T(8,128)(2,1)} %constant.10.clone.ahead_hbm, s32[8]{0:T(128)} %centroid_ref.1), custom_call_target="tpu_custom_call" | custom-call | tf_op jit(solution)/shard_map/turn_and_azimuth/pallas_call | solution.py:372
  47.9 0.0 copy-done
  47.9 2.9 %convolution_convert_fusion = bf16[1024,512]{0,1:T(8,128)(2,1)} fusion(bf16[512,512]{1,0:T(8,128)(2,1)S(1)} %copy-done, bf16[512,1024]{1,0:T(8,128)(2,1)} %turn_and_azimuth.1), kind=kOutput, calls=%fused_computation | convolution fusion | flops 537395200 | bytes 2621440 | tf_op jit(solution)/shard_map/dot_general | solution.py:53
Async XLA Ops:
  7.2 40.7 %copy-start = (bf16[512,512]{1,0:T(8,128)(2,1)S(1)}, bf16[512,512]{1,0:T(8,128)(2,1)}, u32[]{:S(2)}) copy-start(bf16[512,512]{1,0:T(8,128)(2,1)} %constant.11.clone) | copy-start | bytes 1572868

commit v2 on v1

--- a/solution.py
+++ b/solution.py
@@ -60,16 +60,40 @@
     return copies
 
 
-def range_kernel(
-    ranks, group, e_hbm, ref_hbm, mats_hbm, tables_hbm, send_ref,
-    lines, cells, slots, e_ref, ref_ref, mats, tables, sems,
+def turn_kernel(
+    ranks, group, chunk, e_hbm, ref_hbm, tables_hbm, mats_hbm,
+    kernels_hbm, shift_hbm, phase_hbm, az_hbm, ahead_hbm, centroid_ref,
+    out_ref, lines, cells, slots, early_send, late_send, early_got, late_got,
+    doppler, weights, filters, moves, e_ref, ref_ref, tables, mats,
+    kernels_ref, shift_ref, phase_ref, az_ref, ahead, sems, send_sems, got_sems,
 ):
-    pulses = e_ref.shape[1]
-    blocks = R1 // ranks
+    me = lax.axis_index("range")
+    blocks, total = shift_ref.shape
+    pulses = total // ranks
+    taps, phases = kernels_ref.shape
+    lead = taps // 2 - 1
+    chunks = blocks // chunk
+
+    barrier = pltpu.get_barrier_semaphore()
+
+    def greet(k, carry):
+        pl.semaphore_signal(
+            barrier, inc=1, device_id={"range": lax.rem(me + k, ranks)},
+            device_id_type=pl.DeviceIdType.MESH,
+        )
+        return carry
+
+    lax.fori_loop(1, ranks, greet, 0)
     copies = fetch(
-        [(e_hbm, e_ref), (ref_hbm, ref_ref), (tables_hbm, tables), (mats_hbm, mats)], sems
+        [
+            (e_hbm, e_ref), (ref_hbm, ref_ref), (tables_hbm, tables), (mats_hbm, mats),
+            (kernels_hbm, kernels_ref), (shift_hbm, shift_ref), (phase_hbm, phase_ref),
+            (az_hbm, az_ref), (ahead_hbm, ahead),
+        ],
+        sems,
     )
     copies[0].wait()
+    part_pulses = pulses // 2
 
     def spread(n1, carry):
         lane = pl.multiple_of(n1 * RB, RB)
@@ -78,7 +102,7 @@
         return carry
 
     lax.fori_loop(0, R1, spread, 0, unroll=32)
-    for copy in copies[1:]:
+    for copy in copies[1:4]:
         copy.wait()
     for part in range(2):
         for k2 in range(ref_ref.shape[1] // R1):
@@ -137,90 +161,79 @@
                 ]
         return carry
 
-    for g in range(pulses // group):
-        step(g, 0)
-
-    lane = lax.broadcasted_iota(jnp.int32, (pulses, RB), 1)
-    mine = (lane < RB // 4) | (lane >= RB - RB // 4)
+    def transform(h):
+        steps = part_pulses // group
+        for g in range(h * steps, (h + 1) * steps):
+            step(g, 0)
+
+    def pack(h, d, b):
+        begin = (d * blocks + b) * pulses + h * part_pulses
+        return jnp.concatenate(
+            [cells[part, pl.ds(begin, part_pulses), :] for part in range(2)], 0
+        ).astype(BF16)
+
+    def rows(c):
+        if c == 1:
+            return pl.ds(0, pulses + chunk * pulses)
+        return pl.ds(pulses + (c - 1) * chunk * pulses, chunk * pulses)
+
+    def remote(c, to, owner):
+        if c == 0:
+            src, dst = early_send.at[to], early_got.at[owner]
+        else:
+            src, dst = late_send.at[to, rows(c)], late_got.at[owner, rows(c)]
+        return pltpu.make_async_remote_copy(
+            src_ref=src,
+            dst_ref=dst,
+            send_sem=send_sems.at[c, to],
+            recv_sem=got_sems.at[c, owner],
+            device_id={"range": to},
+            device_id_type=pl.DeviceIdType.MESH,
+        )
+
+    half = ranks // 2
+    side = me // half
+
+    def depart(c):
+        def across(k, carry):
+            remote(c, (1 - side) * half + lax.rem(me + k, half), me).start()
+            return carry
+
+        def near(k, carry):
+            remote(c, side * half + lax.rem(me + k, half), me).start()
+            return carry
+
+        lax.fori_loop(0, half, across, 0)
+        lax.fori_loop(1, half, near, 0)
+
+    transform(0)
+    for d in range(ranks):
+        for b in range(blocks):
+            early_send[d, b * pulses : (b + 1) * pulses, :] = pack(0, d, b)
+    pl.semaphore_wait(barrier, ranks - 1)
+    depart(0)
+    own_early = pltpu.make_async_copy(early_send.at[me], early_got.at[me], sems.at[9])
+    own_early.start()
+    transform(1)
+    spot = lax.broadcasted_iota(jnp.int32, (pulses, RB), 1)
+    mine = (spot < RB // 4) | (spot >= RB - RB // 4)
     zero = jnp.zeros((pulses, RB), F32)
-
     for d in range(ranks):
         packed = []
         for part in range(2):
             after = zero if d == ranks - 1 else cells[part, pl.ds((d + 1) * blocks * pulses, pulses), :]
             before = zero if d == 0 else cells[part, pl.ds((d * blocks - 1) * pulses, pulses), :]
-            packed.append(jnp.where(lane < RB // 2, after, before))
-        send_ref[d, :pulses, :] = jnp.where(
+            packed.append(jnp.where(spot < RB // 2, after, before))
+        late_send[d, :pulses, :] = jnp.where(
             mine, packed[0], pltpu.roll(packed[1], RB // 2, 1)
         ).astype(BF16)
         for b in range(blocks):
-            for part in range(2):
-                begin = pulses + (2 * b + part) * pulses
-                send_ref[d, begin : begin + pulses, :] = cells[
-                    part, pl.ds((d * blocks + b) * pulses, pulses), :
-                ].astype(BF16)
-
-
-def turn_kernel(
-    ranks, chunk, send_hbm, kernels_hbm, shift_hbm, phase_hbm, az_hbm, ahead_hbm, centroid_ref,
-    out_ref, got, doppler, weights, filters, moves,
-    kernels_ref, shift_ref, phase_ref, az_ref, ahead, sems, send_sems, got_sems,
-):
-    me = lax.axis_index("range")
-    blocks, total = shift_ref.shape
-    pulses = total // ranks
-    taps, phases = kernels_ref.shape
-    lead = taps // 2 - 1
-    chunks = blocks // chunk
-
-    barrier = pltpu.get_barrier_semaphore()
-
-    def greet(k, carry):
-        pl.semaphore_signal(
-            barrier, inc=1, device_id={"range": lax.rem(me + k, ranks)},
-            device_id_type=pl.DeviceIdType.MESH,
-        )
-        return carry
-
-    lax.fori_loop(1, ranks, greet, 0)
-    copies = fetch(
-        [
-            (kernels_hbm, kernels_ref), (shift_hbm, shift_ref), (phase_hbm, phase_ref),
-            (az_hbm, az_ref), (ahead_hbm, ahead), (send_hbm.at[me], got.at[me]),
-        ],
-        sems,
-    )
-    pl.semaphore_wait(barrier, ranks - 1)
-
-    def rows(c):
-        if c == 0:
-            return pl.ds(0, pulses + 2 * chunk * pulses)
-        return pl.ds(pulses + 2 * c * chunk * pulses, 2 * chunk * pulses)
-
-    def remote(c, to, owner):
-        return pltpu.make_async_remote_copy(
-            src_ref=send_hbm.at[to, rows(c)],
-            dst_ref=got.at[owner, rows(c)],
-            send_sem=send_sems.at[c, to],
-            recv_sem=got_sems.at[c, owner],
-            device_id={"range": to},
-            device_id_type=pl.DeviceIdType.MESH,
-        )
-
-    half = ranks // 2
-
-    def depart(c):
-        def begin(k, carry):
-            remote(c, lax.rem(me + k, ranks), me).start()
-            return carry
-
-        lax.fori_loop(half, ranks, begin, 0)
-        lax.fori_loop(1, half, begin, 0)
-
-    for c in range(min(2, chunks)):
+            late_send[d, (b + 1) * pulses : (b + 2) * pulses, :] = pack(1, d, b)
+    own_late = pltpu.make_async_copy(late_send.at[me], late_got.at[me], sems.at[10])
+    own_late.start()
+    for c in range(1, min(2, chunks) + 1):
         depart(c)
-
-    for copy in copies:
+    for copy in copies[4:]:
         copy.wait()
 
     wide = lax.broadcasted_iota(jnp.int32, (blocks, 1), 0)
@@ -293,30 +306,40 @@
             out_ref[here, cells] = (found[0] * ar - found[1] * ai).astype(BF16)
             out_ref[pl.ds(total + row, size), cells] = (found[0] * ai + found[1] * ar).astype(BF16)
 
-    for c in range(chunks):
-
-        def arrive(k, carry):
+    def arrive(c):
+        def one(k, carry):
             remote(c, me, lax.rem(me + k, ranks)).wait_recv()
             return carry
 
-        lax.fori_loop(1, ranks, arrive, 0)
+        lax.fori_loop(1, ranks, one, 0)
+
+    own_early.wait()
+    own_late.wait()
+    arrive(0)
+    for b in range(blocks):
+        x = early_got[:, b * pulses : (b + 1) * pulses, :].reshape(total, RB)
+        doppler[b + 1] = dot(ahead[0], x)
+    for c in range(chunks):
+        arrive(c + 1)
         if c + 2 < chunks:
-            depart(c + 2)
+            depart(c + 3)
         if c == 0:
-            halo = got[:, :pulses, :]
+            halo = late_got[:, :pulses, :].astype(F32)
             turned = jnp.concatenate([halo[:, :, RB // 2 :], halo[:, :, : RB // 2]], 2)
-            edge = jnp.stack([halo, turned], 1).reshape(2 * total, RB)
-            edge = dot(ahead[...], edge)
+            edge = jnp.zeros((2 * total, RB), F32)
+            for h in range(2):
+                at = slice(h * part_pulses, (h + 1) * part_pulses)
+                x = jnp.concatenate([halo[:, at], turned[:, at]], 1).astype(BF16)
+                edge += dot(ahead[h], x.reshape(total, RB))
             doppler[0] = edge
             doppler[blocks + 1] = edge
         for b in range(c * chunk, (c + 1) * chunk):
-            begin_row = pulses + 2 * b * pulses
-            x = got[:, begin_row : begin_row + 2 * pulses, :].reshape(2 * total, RB)
-            doppler[b + 1] = dot(ahead[...], x)
+            x = late_got[:, (b + 1) * pulses : (b + 2) * pulses, :].reshape(total, RB)
+            doppler[b + 1] += dot(ahead[1], x)
         for b in range(max(c * chunk - 1, 0), (c + 1) * chunk - (c < chunks - 1)):
             focus(b)
 
-    for c in range(chunks):
+    for c in range(chunks + 1):
 
         def leave(k, carry):
             remote(c, lax.rem(me + k, ranks), me).wait_send()
@@ -343,57 +366,51 @@
         pair(twist(R1, second, 1.0) / math.sqrt(samples)),
     ])
     turn = azimuth_matrix(ranks, pulses)
-    ahead = left_matrix(turn).reshape(2 * total, 2, ranks, pulses).transpose(0, 2, 1, 3)
-    ahead = ahead.reshape(2 * total, 2 * total)
+    ahead = left_matrix(turn).reshape(2 * total, 2, ranks, 2, pulses // 2).transpose(3, 0, 2, 1, 4)
+    ahead = ahead.reshape(2, 2 * total, total)
     back = left_matrix(turn.conj().T)
     vmem = pl.BlockSpec(memory_space=pltpu.VMEM)
     anywhere = pl.BlockSpec(memory_space=pl.ANY)
-    height = 2 * blocks * pulses + pulses
     dma = pltpu.SemaphoreType.DMA
-    send = pl.pallas_call(
-        functools.partial(range_kernel, ranks, math.gcd(pulses, 4)),
-        out_shape=jax.ShapeDtypeStruct((ranks, height, RB), BF16),
-        in_specs=[anywhere] * 4,
+    chunk = max(1, blocks // 4)
+    focused = pl.pallas_call(
+        functools.partial(turn_kernel, ranks, math.gcd(pulses // 2, 4), chunk),
+        out_shape=jax.ShapeDtypeStruct((2 * total, blocks * RB), BF16),
+        in_specs=[anywhere] * 9 + [pl.BlockSpec(memory_space=pltpu.SMEM)],
         out_specs=vmem,
         scratch_shapes=[
             pltpu.VMEM((2, R1 * pulses, RB), F32),
             pltpu.VMEM((2, R1 * pulses, RB), F32),
             pltpu.VMEM((2, R1, second), F32),
-            pltpu.VMEM(echoes.shape, BF16),
-            pltpu.VMEM(range_reference.shape, F32),
-            pltpu.VMEM(mats.shape, BF16),
-            pltpu.VMEM(tables.shape, F32),
-            dma((4,)),
-        ],
-        compiler_params=pltpu.CompilerParams(vmem_limit_bytes=VMEM_BYTES),
-        name="range_lines",
-    )(echoes, range_reference, mats, tables)
-    chunk = max(1, blocks // 4)
-    focused = pl.pallas_call(
-        functools.partial(turn_kernel, ranks, chunk),
-        out_shape=jax.ShapeDtypeStruct((2 * total, blocks * RB), BF16),
-        in_specs=[anywhere] * 6 + [pl.BlockSpec(memory_space=pltpu.SMEM)],
-        out_specs=vmem,
-        scratch_shapes=[
-            pltpu.VMEM((ranks, height, RB), BF16),
+            pltpu.VMEM((ranks, blocks * pulses, RB), BF16),
+            pltpu.VMEM((ranks, (blocks + 1) * pulses, RB), BF16),
+            pltpu.VMEM((ranks, blocks * pulses, RB), BF16),
+            pltpu.VMEM((ranks, (blocks + 1) * pulses, RB), BF16),
             pltpu.VMEM((blocks + 2, 2 * total, RB), F32),
             pltpu.VMEM((blocks, taps, total, RB), F32),
             pltpu.VMEM((blocks, 2, total, RB), F32),
             pltpu.VMEM((blocks, total, RB), jnp.int32),
+            pltpu.VMEM(echoes.shape, BF16),
+            pltpu.VMEM(range_reference.shape, F32),
+            pltpu.VMEM(tables.shape, F32),
+            pltpu.VMEM(mats.shape, BF16),
             pltpu.VMEM(kernels.shape[::-1], F32),
             pltpu.VMEM(shifts.shape, jnp.int32),
             pltpu.VMEM(shifts.shape, jnp.int32),
             pltpu.VMEM(azimuth_reference.shape, F32),
             pltpu.VMEM(ahead.shape, BF16),
-            dma((6,)),
-            dma((blocks // chunk, ranks)),
-            dma((blocks // chunk, ranks)),
+            dma((11,)),
+            dma((blocks // chunk + 1, ranks)),
+            dma((blocks // chunk + 1, ranks)),
         ],
         compiler_params=pltpu.CompilerParams(
             vmem_limit_bytes=VMEM_BYTES, collective_id=0, has_side_effects=True
         ),
         name="turn_and_azimuth",
-    )(send, kernels.T, shifts, phase_index, azimuth_reference, ahead, centroid)
+    )(
+        echoes, range_reference, tables, mats, kernels.T, shifts, phase_index, azimuth_reference,
+        ahead, centroid,
+    )
     return dot(back, focused).astype(BF16).reshape(2, total, blocks * RB)
 
 

time: 51 us -> 49.5 us (0.971)
  Pallas kernels: 47.8 us -> 46.3 us
    pallas_call x2 -> x1, Pallas kernels: 47.8 us -> 46.3 us  [local(): pl.pallas_call(functools.partial(turn_kernel, ranks, math.gcd(pulses // 2...]
where the time goes in v2:
time: 49.5 us; the launch traced here: 49.3 us
  Pallas kernels  46.3 us (94%)
  matrix products  2.91 us (6%)
    pallas_call x1, Pallas kernels, local(): pl.pallas_call(functools.partial(turn_kernel, ranks, math.gcd(pulses // 2...  46.3 us
    dot_general x1, matrix products, dot(): return jnp.dot(a, b, preferred_element_type=F32)  2.91 us

profile of v2, /device:TPU:0, one launch (start us, length us, event | category | flops | bytes accessed | tf_op | source)
XLA Modules:
  0.0 49.3 jit_solution(14675926613065966130)
XLA Ops:
  0.0 0.0 copy-start
  0.0 46.3 %turn_and_azimuth.1 = bf16[512,1024]{1,0:T(8,128)(2,1)} custom-call(bf16[2,16,16384]{2,1,0:T(8,128)(2,1)} %e_hbm.1, f32[2,16384]{1,0:T(2,128)} %ref_hbm.1, f32[4,128,128]{2,1,0:T(8,128)} %constant.8.clone.tables_hbm, bf16[4,256,256]{2,1,0:T(8,128)(2,1)} %constant.9.clone.mats_hbm, f32[8,16]{1,0:T(8,128)} %bitcast.6, s32[8,256]{1,0:T(8,128)} %shift_hbm.1, ...), custom_call_target="tpu_custom_call" | custom-call | tf_op jit(solution)/shard_map/turn_and_azimuth/pallas_call | solution.py:376
  46.3 0.0 copy-done
  46.4 2.9 %convolution_convert_fusion = bf16[1024,512]{0,1:T(8,128)(2,1)} fusion(bf16[512,512]{1,0:T(8,128)(2,1)S(1)} %copy-done, bf16[512,1024]{1,0:T(8,128)(2,1)} %turn_and_azimuth.1), kind=kOutput, calls=%fused_computation | convolution fusion | flops 537395200 | bytes 2621440 | tf_op jit(solution)/shard_map/dot_general | solution.py:53
Async XLA Ops:
  0.0 46.3 %copy-start = (bf16[512,512]{1,0:T(8,128)(2,1)S(1)}, bf16[512,512]{1,0:T(8,128)(2,1)}, u32[]{:S(2)}) copy-start(bf16[512,512]{1,0:T(8,128)(2,1)} %constant.11.clone) | copy-start | bytes 1572868

commit v3 on v2

--- a/solution.py
+++ b/solution.py
@@ -61,7 +61,7 @@
 
 
 def turn_kernel(
-    ranks, group, chunk, e_hbm, ref_hbm, tables_hbm, mats_hbm,
+    ranks, group, sizes, e_hbm, ref_hbm, tables_hbm, mats_hbm,
     kernels_hbm, shift_hbm, phase_hbm, az_hbm, ahead_hbm, centroid_ref,
     out_ref, lines, cells, slots, early_send, late_send, early_got, late_got,
     doppler, weights, filters, moves, e_ref, ref_ref, tables, mats,
@@ -72,7 +72,8 @@
     pulses = total // ranks
     taps, phases = kernels_ref.shape
     lead = taps // 2 - 1
-    chunks = blocks // chunk
+    chunks = len(sizes)
+    starts = [sum(sizes[:c]) for c in range(chunks + 1)]
 
     barrier = pltpu.get_barrier_semaphore()
 
@@ -92,23 +93,28 @@
         ],
         sems,
     )
-    copies[0].wait()
     part_pulses = pulses // 2
 
-    def spread(n1, carry):
-        lane = pl.multiple_of(n1 * RB, RB)
-        for part in range(2):
-            lines[part, pl.ds(n1, pulses, stride=R1), :] = e_ref[part, :, pl.ds(lane, RB)].astype(F32)
-        return carry
-
-    lax.fori_loop(0, R1, spread, 0, unroll=32)
-    for copy in copies[1:4]:
-        copy.wait()
+    copies[1].wait()
     for part in range(2):
         for k2 in range(ref_ref.shape[1] // R1):
             slots[part, k2 : k2 + 1, :] = ref_ref[part : part + 1, k2 * R1 : (k2 + 1) * R1]
     for part in range(2):
         slots[part] = slots[part].T
+    for copy in (copies[2], copies[3], copies[0]):
+        copy.wait()
+
+    def spread(h):
+        def one(n1, carry):
+            lane = pl.multiple_of(n1 * RB, RB)
+            for part in range(2):
+                tile = e_ref[part, :, pl.ds(lane, RB)].astype(F32)
+                lines[part, pl.ds(h * part_pulses * R1 + n1, part_pulses, stride=R1), :] = tile[
+                    h * part_pulses : (h + 1) * part_pulses
+                ]
+            return carry
+
+        lax.fori_loop(0, R1, one, 0, unroll=32)
 
     def times(re, im, tr, ti):
         return (re * tr - im * ti).astype(BF16), (re * ti + im * tr).astype(BF16)
@@ -162,6 +168,7 @@
         return carry
 
     def transform(h):
+        spread(h)
         steps = part_pulses // group
         for g in range(h * steps, (h + 1) * steps):
             step(g, 0)
@@ -174,8 +181,8 @@
 
     def rows(c):
         if c == 1:
-            return pl.ds(0, pulses + chunk * pulses)
-        return pl.ds(pulses + (c - 1) * chunk * pulses, chunk * pulses)
+            return pl.ds(0, pulses + sizes[0] * pulses)
+        return pl.ds(pulses + starts[c - 1] * pulses, sizes[c - 1] * pulses)
 
     def remote(c, to, owner):
         if c == 0:
@@ -231,7 +238,7 @@
             late_send[d, (b + 1) * pulses : (b + 2) * pulses, :] = pack(1, d, b)
     own_late = pltpu.make_async_copy(late_send.at[me], late_got.at[me], sems.at[10])
     own_late.start()
-    for c in range(1, min(2, chunks) + 1):
+    for c in range(1, min(3, chunks) + 1):
         depart(c)
     for copy in copies[4:]:
         copy.wait()
@@ -321,8 +328,8 @@
         doppler[b + 1] = dot(ahead[0], x)
     for c in range(chunks):
         arrive(c + 1)
-        if c + 2 < chunks:
-            depart(c + 3)
+        if c + 3 < chunks:
+            depart(c + 4)
         if c == 0:
             halo = late_got[:, :pulses, :].astype(F32)
             turned = jnp.concatenate([halo[:, :, RB // 2 :], halo[:, :, : RB // 2]], 2)
@@ -333,10 +340,10 @@
                 edge += dot(ahead[h], x.reshape(total, RB))
             doppler[0] = edge
             doppler[blocks + 1] = edge
-        for b in range(c * chunk, (c + 1) * chunk):
+        for b in range(starts[c], starts[c + 1]):
             x = late_got[:, (b + 1) * pulses : (b + 2) * pulses, :].reshape(total, RB)
             doppler[b + 1] += dot(ahead[1], x)
-        for b in range(max(c * chunk - 1, 0), (c + 1) * chunk - (c < chunks - 1)):
+        for b in range(max(starts[c] - 1, 0), starts[c + 1] - (c < chunks - 1)):
             focus(b)
 
     for c in range(chunks + 1):
@@ -372,9 +379,11 @@
     vmem = pl.BlockSpec(memory_space=pltpu.VMEM)
     anywhere = pl.BlockSpec(memory_space=pl.ANY)
     dma = pltpu.SemaphoreType.DMA
-    chunk = max(1, blocks // 4)
+    rest = blocks - 1
+    parts = min(3, rest)
+    sizes = tuple(rest // parts + (i < rest % parts) for i in range(parts)) + (1,)
     focused = pl.pallas_call(
-        functools.partial(turn_kernel, ranks, math.gcd(pulses // 2, 4), chunk),
+        functools.partial(turn_kernel, ranks, math.gcd(pulses // 2, 4), sizes),
         out_shape=jax.ShapeDtypeStruct((2 * total, blocks * RB), BF16),
         in_specs=[anywhere] * 9 + [pl.BlockSpec(memory_space=pltpu.SMEM)],
         out_specs=vmem,
@@ -400,8 +409,8 @@
             pltpu.VMEM(azimuth_reference.shape, F32),
             pltpu.VMEM(ahead.shape, BF16),
             dma((11,)),
-            dma((blocks // chunk + 1, ranks)),
-            dma((blocks // chunk + 1, ranks)),
+            dma((len(sizes) + 1, ranks)),
+            dma((len(sizes) + 1, ranks)),
         ],
         compiler_params=pltpu.CompilerParams(
             vmem_limit_bytes=VMEM_BYTES, collective_id=0, has_side_effects=True

time: 49.5 us -> 50.6 us (1.022)
  Pallas kernels: 46.3 us -> 47.5 us
    pallas_call x1, Pallas kernels: 46.3 us -> 47.5 us  [local(): pl.pallas_call(functools.partial(turn_kernel, ranks, math.gcd(pulses // 2...]
where the time goes in v3:
time: 50.6 us; the launch traced here: 50.4 us
  Pallas kernels  47.5 us (94%)
  matrix products  2.91 us (6%)
    pallas_call x1, Pallas kernels, local(): pl.pallas_call(functools.partial(turn_kernel, ranks, math.gcd(pulses // 2...  47.5 us
    dot_general x1, matrix products, dot(): return jnp.dot(a, b, preferred_element_type=F32)  2.91 us

profile of v3, /device:TPU:0, one launch (start us, length us, event | category | flops | bytes accessed | tf_op | source)
XLA Modules:
  0.0 50.4 jit_solution(2126876969862006906)
XLA Ops:
  0.0 0.0 copy-start
  0.0 47.5 %turn_and_azimuth.1 = bf16[512,1024]{1,0:T(8,128)(2,1)} custom-call(bf16[2,16,16384]{2,1,0:T(8,128)(2,1)} %e_hbm.1, f32[2,16384]{1,0:T(2,128)} %ref_hbm.1, f32[4,128,128]{2,1,0:T(8,128)} %constant.8.clone.tables_hbm, bf16[4,256,256]{2,1,0:T(8,128)(2,1)} %constant.9.clone.mats_hbm, f32[8,16]{1,0:T(8,128)} %bitcast.6, s32[8,256]{1,0:T(8,128)} %shift_hbm.1, ...), custom_call_target="tpu_custom_call" | custom-call | tf_op jit(solution)/shard_map/turn_and_azimuth/pallas_call | solution.py:385
  47.5 0.0 copy-done
  47.5 2.9 %convolution_convert_fusion = bf16[1024,512]{0,1:T(8,128)(2,1)} fusion(bf16[512,512]{1,0:T(8,128)(2,1)S(1)} %copy-done, bf16[512,1024]{1,0:T(8,128)(2,1)} %turn_and_azimuth.1), kind=kOutput, calls=%fused_computation | convolution fusion | flops 537395200 | bytes 2621440 | tf_op jit(solution)/shard_map/dot_general | solution.py:53
Async XLA Ops:
  0.0 47.5 %copy-start = (bf16[512,512]{1,0:T(8,128)(2,1)S(1)}, bf16[512,512]{1,0:T(8,128)(2,1)}, u32[]{:S(2)}) copy-start(bf16[512,512]{1,0:T(8,128)(2,1)} %constant.11.clone) | copy-start | bytes 1572868
